TPU v7x, 32 devices: a whole 2x2x4 slice. The times are simulated.
32 devices in a mesh: row: 4 (over z), col: 8 (over y, x, core).
Axes of the slice: x: 2, y: 2, z: 4, core: 2. Of those that a mesh axis runs over, the one named last changes fastest.
Arguments:
- object_field: float32 [2, 4, 1024, 2048], P(None, None, 'row', 'col'), may hold values from -4 to 4
- probe: float32 [2, 4, 128, 128], replicated, may hold values from -6 to 6
- amplitudes: float32 [4, 8, 5, 128, 128], P('row', 'col'), may hold values from 0.2 to 4
- offsets: int32 [4, 8, 5, 2], P('row', 'col'), may hold values from 0 to 1920, as said below
- counts: int32 [4, 8], P('row', 'col'), may hold values from 1 to 5, as said below
Outputs:
- new_object: float32 [2, 4, 1024, 2048], P(None, None, 'row', 'col')
- new_probe: float32 [2, 4, 128, 128], replicated
Inputs may be any that keep to these rules, and one draw needn't show every extreme that they name: `offsets`: slot k of device (a, b) has corner (y, x) with a * 256 <= y < (a + 1) * 256, b * 256 <= x < (b + 1) * 256, y <= 896 and x <= 1920; dead slots hold such corners too. Slots k >= counts of a device are dead; some device has all 5 slots live.
All inputs are finite; a program needn't handle non-finite values.
Results may differ from a plain program's by a relative error of at most 0.00019.
Values sent between devices are 32-bit elements; how exact they have to be, the bound alone decides.
A program may use at most 128 MiB of HBM per device.

v0:
```python
from functools import partial
import math

import jax
import jax.numpy as jnp
from jax import lax
from jax.sharding import PartitionSpec as P

FRESNEL = 4.0
STEP_OBJECT = 0.5
STEP_PROBE = 0.5


def shifted(value, axis, steps):
    count = lax.axis_size(axis)
    leading, last = (max(0, -steps), min(count, count - steps))
    return lax.ppermute(value, axis, [(source, source + steps) for source in range(leading, last)])


def dft_tables(points):
    position = jnp.arange(points, dtype=jnp.int32)
    product = position[:, None] * position[None, :] % points
    angle = -2.0 * math.pi / points * product.astype(jnp.float32)
    norm_factor = 1.0 / math.sqrt(points)
    frequency = (
        jnp.where(position < points // 2, position, position - points).astype(jnp.float32) / points
    )
    phase = -math.pi * FRESNEL * (frequency[:, None] ** 2 + frequency[None, :] ** 2)
    return (
        jnp.cos(angle) * norm_factor,
        jnp.sin(angle) * norm_factor,
        jnp.cos(phase),
        jnp.sin(phase),
    )


def product_left(table_real, table_imag, field_real, field_imag):
    contract = partial(jnp.einsum, precision=lax.Precision.HIGHEST)
    real_part = contract("jk,mkl->mjl", table_real, field_real) - contract(
        "jk,mkl->mjl", table_imag, field_imag
    )
    imag_part = contract("jk,mkl->mjl", table_real, field_imag) + contract(
        "jk,mkl->mjl", table_imag, field_real
    )
    return (real_part, imag_part)


def product_right(field_real, field_imag, table_real, table_imag):
    contract = partial(jnp.einsum, precision=lax.Precision.HIGHEST)
    real_part = contract("mjk,kl->mjl", field_real, table_real) - contract(
        "mjk,kl->mjl", field_imag, table_imag
    )
    imag_part = contract("mjk,kl->mjl", field_real, table_imag) + contract(
        "mjk,kl->mjl", field_imag, table_real
    )
    return (real_part, imag_part)


def transform(field_real, field_imag, table_real, table_imag):
    mixed_real, mixed_imag = product_left(table_real, table_imag, field_real, field_imag)
    return product_right(mixed_real, mixed_imag, table_real, table_imag)


def position_loss(window, probe, amplitude, tables):
    table_real, table_imag, kernel_real, kernel_imag = tables
    wave_real = probe[0]
    wave_imag = probe[1]
    depth = window.shape[1]
    for slice_index in range(depth):
        object_real = window[0, slice_index]
        object_imag = window[1, slice_index]
        wave_real, wave_imag = (
            wave_real * object_real - wave_imag * object_imag,
            wave_real * object_imag + wave_imag * object_real,
        )
        if slice_index < depth - 1:
            spec_real, spec_imag = transform(wave_real, wave_imag, table_real, table_imag)
            spec_real, spec_imag = (
                spec_real * kernel_real - spec_imag * kernel_imag,
                spec_real * kernel_imag + spec_imag * kernel_real,
            )
            wave_real, wave_imag = transform(spec_real, spec_imag, table_real, -table_imag)
    far_real, far_imag = transform(wave_real, wave_imag, table_real, table_imag)
    intensity = jnp.sum(far_real**2 + far_imag**2, axis=0)
    return jnp.sum((jnp.sqrt(intensity + 1.0) - amplitude) ** 2)


def shards(object_field, probe, amplitudes, offsets, counts):
    tile_rows = object_field.shape[2]
    tile_cols = object_field.shape[3]
    depth = object_field.shape[1]
    points = probe.shape[2]
    slot_count = offsets.shape[2]
    row_index = lax.axis_index("row")
    col_index = lax.axis_index("col")
    below = shifted(object_field[:, :, :points, :], "row", -1)
    rows_extended = jnp.concatenate([object_field, below], axis=2)
    right_rim = shifted(rows_extended[:, :, :, :points], "col", -1)
    extended = jnp.concatenate([rows_extended, right_rim], axis=3)
    tables = dft_tables(points)
    local_rows = offsets[0, 0, :, 0] - row_index * tile_rows
    local_cols = offsets[0, 0, :, 1] - col_index * tile_cols

    def cut_window(start_row, start_col):
        return lax.dynamic_slice(extended, (0, 0, start_row, start_col), (2, depth, points, points))

    windows = jax.vmap(cut_window)(local_rows, local_cols)
    alive = (jnp.arange(slot_count, dtype=jnp.int32) < counts[0, 0]).astype(jnp.float32)
    target = amplitudes[0, 0]

    def total_loss(window_batch, probe_part):
        losses = jax.vmap(position_loss, in_axes=(0, None, 0, None))(
            window_batch, probe_part, target, tables
        )
        return jnp.sum(alive * losses)

    loss_value, pull_back = jax.vjp(total_loss, windows, probe)
    grad_windows, grad_probe = pull_back(jnp.ones((), jnp.float32))
    weight = jnp.sum(alive[:, None, None] * (windows[:, 0, 0] ** 2 + windows[:, 1, 0] ** 2), axis=0)
    grad_ext = jnp.zeros((2, depth, tile_rows + points, tile_cols + points), jnp.float32)
    for slot_index in range(slot_count):
        starts = (0, 0, local_rows[slot_index], local_cols[slot_index])
        previous = lax.dynamic_slice(grad_ext, starts, (2, depth, points, points))
        grad_ext = lax.dynamic_update_slice(grad_ext, previous + grad_windows[slot_index], starts)
    returned = shifted(grad_ext[:, :, :, tile_cols:], "col", 1)
    grad_ext = grad_ext.at[:, :, :, :points].add(returned)
    lower_back = shifted(grad_ext[:, :, tile_rows:, :tile_cols], "row", 1)
    grad_tile = grad_ext[:, :, :tile_rows, :tile_cols].at[:, :, :points, :].add(lower_back)
    new_object = object_field - STEP_OBJECT * grad_tile
    grad_total, weight_total = lax.psum((grad_probe, weight), ("row", "col"))
    new_probe = probe - STEP_PROBE * grad_total / (weight_total + 1.0)
    return (new_object, new_probe)


def solution(mesh):
    return jax.shard_map(
        shards,
        mesh=mesh,
        in_specs=(
            P(None, None, "row", "col"),
            P(),
            P("row", "col", None, None, None),
            P("row", "col", None, None),
            P("row", "col"),
        ),
        out_specs=(P(None, None, "row", "col"), P()),
        check_vma=False,
    )
```

profile of v0, /device:TPU:1, one launch (start us, length us, event | category | flops | bytes accessed | tf_op | source)
XLA Modules:
  0.0 557.1 jit_solution(15477752317589711193)
XLA Ops:
  10.1 25.5 %collective-permute-done = f32[2,4,128,256]{3,2,1,0:T(8,128)S(1)} collective-permute-done((f32[2,4,128,256]{3,2,1,0:T(8,128)S(1)}, f32[2,4,128,256]{3,2,1,0:T(8,128)S(1)}, u32[]{:S(2)}, u32[]{:S(2)}) %collective-permute-start) | collective-permute-done | bytes 1048608 | tf_op jit(solution)/shard_map/ppermute | solution.py:17
  36.9 3.1 collective-permute-start.1
  65.3 3.9 pad_maximum_fusion
  69.2 21.4 %while.3 = (s32[]{:T(128)}, f32[2,4,384,384]{3,2,1,0:T(8,128)}, s32[5,4]{0,1:T(4,128)S(1)}, f32[5,2,4,128,128]{4,3,2,1,0:T(8,128)}, s32[]{:T(128)}) while((s32[]{:T(128)}, f32[2,4,384,384]{3,2,1,0:T(8,128)}, s32[5,4]{0,1:T(4,128)S(1)}, f32[5,2,4,128,128]{4,3,2,1,0:T(8,128)}, s32[]{:T(128)}) %tuple.86), condition=%wide.while_cond.2, body=%wide.while_body.2.sunk | while | flops 2 | bytes 1049725 | solution.py:105
  69.8 3.6 bitcast_dynamic-update-slice_fusion.2
  74.0 3.6 bitcast_dynamic-update-slice_fusion.2
  78.2 3.6 bitcast_dynamic-update-slice_fusion.2
  82.3 3.6 bitcast_dynamic-update-slice_fusion.2
  86.5 3.6 bitcast_dynamic-update-slice_fusion.2
  118.6 2.6 fusion.142
  130.8 2.9 fusion.106
  143.5 2.7 fusion.6
  156.0 2.7 fusion.7
  168.3 2.8 convolution_subtract_fusion.6
  181.0 2.6 fusion.237
  193.4 2.7 fusion.94
  205.9 2.8 convolution_add_fusion.30
  218.4 2.6 fusion.225
  241.8 3.5 multiply_reduce_fusion.18
  269.0 3.0 multiply_reduce_fusion.14
  295.8 3.1 multiply_reduce_fusion.10
  318.5 2.8 fusion.189
  325.2 4.2 multiply_reduce_fusion.3
  337.6 7.8 %dynamic_update_slice.15 = f32[2,4,384,384]{3,2,1,0:T(8,128)} dynamic-update-slice(f32[2,4,384,384]{3,2,1,0:T(8,128)} %broadcast_in_dim.2, f32[2,4,128,128]{3,2,1,0:T(8,128)S(1)} %slice_bitcast_fusion.4, s32[]{:T(128)} %constant.94.clone.1, s32[]{:T(128)} %constant.94.clone.1, s32[]{:T(128)S(6)} %select_n.349, s32[]{:T(128)S(6)} %select_n.350) | dynamic-update-slice | bytes 1048580 | tf_op jit(solution)/shard_map/dynamic_update_slice | solution.py:124
  346.8 7.7 %dynamic_update_slice.16 = f32[2,4,384,384]{3,2,1,0:T(8,128)} dynamic-update-slice(f32[2,4,384,384]{3,2,1,0:T(8,128)} %dynamic_update_slice.15, f32[2,4,128,128]{3,2,1,0:T(8,128)S(1)} %fusion.89, s32[]{:T(128)} %constant.94.clone.1, s32[]{:T(128)} %constant.94.clone.1, s32[]{:T(128)S(6)} %select_n.351, s32[]{:T(128)S(6)} %select_n.352) | dynamic-update-slice | bytes 1048580 | tf_op jit(solution)/shard_map/dynamic_update_slice | solution.py:124
  356.0 6.9 %dynamic_update_slice.17 = f32[2,4,384,384]{3,2,1,0:T(8,128)} dynamic-update-slice(f32[2,4,384,384]{3,2,1,0:T(8,128)} %dynamic_update_slice.16, f32[2,4,128,128]{3,2,1,0:T(8,128)S(1)} %fusion.88, s32[]{:T(128)} %constant.94.clone.1, s32[]{:T(128)} %constant.94.clone.1, s32[]{:T(128)S(6)} %select_n.353, s32[]{:T(128)S(6)} %select_n.354) | dynamic-update-slice | bytes 1048580 | tf_op jit(solution)/shard_map/dynamic_update_slice | solution.py:124
  364.4 7.6 %dynamic_update_slice.18 = f32[2,4,384,384]{3,2,1,0:T(8,128)} dynamic-update-slice(f32[2,4,384,384]{3,2,1,0:T(8,128)} %dynamic_update_slice.17, f32[2,4,128,128]{3,2,1,0:T(8,128)S(1)} %fusion.87, s32[]{:T(128)} %constant.94.clone.1, s32[]{:T(128)} %constant.94.clone.1, s32[]{:T(128)S(6)} %select_n.355, s32[]{:T(128)S(6)} %select_n.356) | dynamic-update-slice | bytes 1048580 | tf_op jit(solution)/shard_map/dynamic_update_slice | solution.py:124
  373.6 7.8 %dynamic_update_slice.19 = f32[2,4,384,384]{3,2,1,0:T(8,128)} dynamic-update-slice(f32[2,4,384,384]{3,2,1,0:T(8,128)} %dynamic_update_slice.18, f32[2,4,128,128]{3,2,1,0:T(8,128)S(1)} %fusion.86, s32[]{:T(128)} %constant.94.clone.1, s32[]{:T(128)} %constant.94.clone.1, s32[]{:T(128)S(6)} %select_n.357, s32[]{:T(128)S(6)} %select_n.358) | dynamic-update-slice | bytes 1048580 | tf_op jit(solution)/shard_map/dynamic_update_slice | solution.py:124
  383.1 4.1 collective-permute-start.2
  387.3 17.2 %collective-permute-done.2 = f32[2,4,384,128]{3,2,1,0:T(8,128)S(1)} collective-permute-done((f32[2,4,384,128]{3,2,1,0:T(8,128)S(1)}, f32[2,4,384,128]{3,2,1,0:T(8,128)S(1)}, u32[]{:S(2)}, u32[]{:S(2)}) %collective-permute-start.2) | collective-permute-done | bytes 1572896 | tf_op jit(solution)/shard_map/ppermute | solution.py:17
  407.1 2.9 collective-permute-start.3
  412.9 128.6 %all-reduce.13.cloned.1.call-done = (f32[2,4,128,128]{2,3,1,0:T(8,128)}, f32[128,128]{1,0:T(8,128)}) async-done(((f32[2,4,128,128]{2,3,1,0:T(8,128)}, f32[128,128]{1,0:T(8,128)}), (f32[2,4,128,128]{2,3,1,0:T(8,128)}, f32[128,128]{1,0:T(8,128)})) %all-reduce.13.cloned.1.call-update) | async-done | bytes 589840 | tf_op jit(solution)/shard_map/psum | solution.py:130
  (218 shorter events, 239.8 us)
Async XLA Ops:
  7.2 534.4 %all-reduce.13.cloned.1.call-start = ((), (), s32[]{:S(2)}) async-start(), calls=%async_computation | async-start | bytes 1179648 | tf_op jit(solution)/shard_map/psum | solution.py:130
  7.2 2.8 copy-start.2
  8.7 26.9 %collective-permute-start = (f32[2,4,128,256]{3,2,1,0:T(8,128)S(1)}, f32[2,4,128,256]{3,2,1,0:T(8,128)S(1)}, u32[]{:S(2)}, u32[]{:S(2)}) collective-permute-start(f32[2,4,128,256]{3,2,1,0:T(8,128)S(1)} %slice.168), channel_id=1, source_target_pairs={{8,0},{16,8},{24,16},{9,1},{17,9},{25,17},{10,2},{18,10},{26,18},{... | collective-permute-start | bytes 3145736 | tf_op jit(solution)/shard_map/ppermute | solution.py:17
  35.7 4.4 copy-start.26
  36.9 28.4 %collective-permute-start.1 = (f32[2,4,384,128]{3,2,1,0:T(8,128)}, f32[2,4,384,128]{3,2,1,0:T(8,128)}, u32[]{:S(2)}, u32[]{:S(2)}) collective-permute-start(f32[2,4,384,128]{3,2,1,0:T(8,128)} %slice.220), channel_id=1, source_target_pairs={{1,0},{2,1},{3,2},{4,3},{5,4},{6,5},{7,6},{9,8},{10,9},{11,10},{12... | collective-permute-start | bytes 4718600 | tf_op jit(solution)/shard_map/ppermute | solution.py:17
  94.1 1.3 copy-start.4
  228.3 2.5 copy-start.25
  329.4 3.6 copy-start.6
  329.4 3.6 copy-start.7
  329.4 3.6 copy-start.8
  329.4 3.6 copy-start.9
  332.0 1.0 copy-start.10
  332.0 1.1 copy-start.11
  332.0 1.3 copy-start.12
  333.0 1.0 copy-start.13
  333.0 1.1 copy-start.14
  333.1 1.2 copy-start.15
  333.1 1.3 copy-start.16
  333.4 1.1 copy-start.17
  333.4 1.2 copy-start.18
  333.4 1.3 copy-start.19
  333.4 1.4 copy-start.20
  373.6 13.6 %copy-start.21 = (f32[4,128,128]{1,2,0:T(8,128)S(1)}, f32[4,128,128]{1,2,0:T(8,128)}, u32[]{:S(2)}) copy-start(f32[4,128,128]{1,2,0:T(8,128)} %get-tuple-element.42) | copy-start | bytes 786436
  373.6 13.6 %copy-start.22 = (f32[4,128,128]{1,2,0:T(8,128)S(1)}, f32[4,128,128]{1,2,0:T(8,128)}, u32[]{:S(2)}) copy-start(f32[4,128,128]{1,2,0:T(8,128)} %get-tuple-element.43) | copy-start | bytes 786436
  373.6 13.6 %copy-start.23 = (f32[4,128,128]{1,2,0:T(8,128)S(1)}, f32[4,128,128]{1,2,0:T(8,128)}, u32[]{:S(2)}) copy-start(f32[4,128,128]{1,2,0:T(8,128)} %get-tuple-element.60) | copy-start | bytes 786436
  373.6 13.6 %copy-start.24 = (f32[4,128,128]{1,2,0:T(8,128)S(1)}, f32[4,128,128]{1,2,0:T(8,128)}, u32[]{:S(2)}) copy-start(f32[4,128,128]{1,2,0:T(8,128)} %get-tuple-element.61) | copy-start | bytes 786436
  381.4 23.1 %copy-start = (f32[2,4,384,384]{3,2,1,0:T(8,128)S(1)}, f32[2,4,384,384]{3,2,1,0:T(8,128)}, u32[]{:S(2)}) copy-start(f32[2,4,384,384]{3,2,1,0:T(8,128)} %dynamic_update_slice.19) | copy-start | bytes 14155780
  383.1 21.5 %collective-permute-start.2 = (f32[2,4,384,128]{3,2,1,0:T(8,128)S(1)}, f32[2,4,384,128]{3,2,1,0:T(8,128)S(1)}, u32[]{:S(2)}, u32[]{:S(2)}) collective-permute-start(f32[2,4,384,128]{3,2,1,0:T(8,128)S(1)} %slice.228), channel_id=1, source_target_pairs={{0,1},{1,2},{2,3},{3,4},{4,5},{5,6},{6,7},{8,9},{9,10},{10,11},{11... | collective-permute-start | bytes 4718600 | tf_op jit(solution)/shard_map/ppermute | solution.py:17
  404.9 2.1 copy-start.1
  407.1 5.6 %copy-start.5 = (f32[2,4,128,128]{3,2,1,0:T(8,128)S(1)}, f32[2,4,128,128]{3,2,1,0:T(8,128)}, u32[]{:S(2)}) copy-start(f32[2,4,128,128]{3,2,1,0:T(8,128)} %param.10) | copy-start | bytes 1572868
  407.1 139.4 %collective-permute-start.3 = (f32[2,4,128,256]{3,2,1,0:T(8,128)S(1)}, f32[2,4,128,256]{3,2,1,0:T(8,128)S(1)}, u32[]{:S(2)}, u32[]{:S(2)}) collective-permute-start(f32[2,4,128,256]{3,2,1,0:T(8,128)S(1)} %slice.231), channel_id=1, source_target_pairs={{0,8},{8,16},{16,24},{1,9},{9,17},{17,25},{2,10},{10,18},{18,26},{... | collective-permute-start | bytes 3145736 | tf_op jit(solution)/shard_map/ppermute | solution.py:17
  546.5 1.9 copy-start.3
Sparse Core Ops, SparseCore 0:
  412.8 128.6 all-reduce.12
where the time goes:
time: 562 us; the launch traced here: 557 us
  matrix products  233 us (41%)
  waiting for transfers between devices  171 us (30%)
  local copies, waits for them, and re-layouts  86.9 us (15%)
  between operations  35 us (6%)
  other arithmetic  19.2 us (3%)
  starting transfers between devices  11.5 us (2%)
    psum x1, waiting for transfers between devices, shards(): grad_total, weight_total = lax.psum((grad_probe, weight), ('row', 'col'))  129 us
    ppermute x4, waiting for transfers between devices, shifted(): lax.ppermute(value, axis, [(source, source + steps) for source in range(l...  42.7 us
    dynamic_update_slice x5, local copies, waits for them, and re-layouts, shards(): lax.dynamic_update_slice(grad_ext, previous + grad_windows[slot_index], s...  37.9 us
    dot_general x14, matrix products, product_left(): contract('jk,mkl->mjl', table_real, field_real)  33.5 us
    dot_general x14, matrix products, product_left(): contract('jk,mkl->mjl', table_imag, field_imag)  31.1 us
    dot_general x14, matrix products, product_left(): contract('jk,mkl->mjl', table_real, field_imag)  28.9 us
    dot_general x14, matrix products, product_left(): contract('jk,mkl->mjl', table_imag, field_real)  28.5 us
    dot_general x14, matrix products, product_right(): contract('mjk,kl->mjl', field_real, table_real)  27.9 us
  transfers between devices with their start and end apart: 5, of which 3 were waited for; matrix products, arithmetic and copies ran while one was open for 2% of the time, Pallas kernels for 0%

commit v1 on v0

v1 whole, which is shorter than its diff:
```python
from functools import partial
import math

import jax
import jax.numpy as jnp
import ml_dtypes
import numpy as np
from jax import lax
from jax.experimental import pallas as pl
from jax.experimental.pallas import tpu as pltpu
from jax.sharding import PartitionSpec as P

FRESNEL = 4.0
STEP_OBJECT = 0.5
STEP_PROBE = 0.5
ROWS = 8


def tables(points):
    position = np.arange(points)
    angle = -2.0 * np.pi / points * (position[:, None] * position[None, :] % points)
    dft = np.exp(1j * angle) / math.sqrt(points)
    frequency = np.where(position < points // 2, position, position - points) / points
    propagator = np.conj(dft) @ (np.exp(-1j * np.pi * FRESNEL * frequency**2)[:, None] * dft)

    def split(matrix):
        high = matrix.astype(np.float32).astype(ml_dtypes.bfloat16)
        low = (matrix - high.astype(np.float64)).astype(np.float32).astype(ml_dtypes.bfloat16)
        return high, low

    lefts, rights = [], []
    for matrix in (propagator, np.conj(propagator), dft, np.conj(dft)):
        real, imag = matrix.real, matrix.imag
        high, low = split(np.block([[real, -imag], [imag, real]]))
        lefts.append(np.concatenate([high, high, low], axis=1))
        high, low = split(np.block([[real, imag], [-imag, real]]))
        rights.append(np.concatenate([high, high, low], axis=0))
    return np.stack(lefts), np.stack(rights)


def split(value):
    high = value.astype(jnp.bfloat16)
    return high, (value - high.astype(jnp.float32)).astype(jnp.bfloat16)


def grid(blocks):
    return jnp.concatenate([jnp.concatenate(row, axis=1) for row in blocks], axis=0)


def left_product(weight, pair):
    n = pair[0].shape[0]
    (r0, r0l), (r1, r1l), (i0, i0l), (i1, i1l) = map(split, pair)
    x = grid([[r0, r1], [i0, i1], [r0l, r1l], [i0l, i1l], [r0, r1], [i0, i1]])
    y = jnp.dot(weight, x, preferred_element_type=jnp.float32)
    return y[:n, :n], y[:n, n:], y[n:, :n], y[n:, n:]


def right_product(weight, pair):
    n = pair[0].shape[0]
    (r0, r0l), (r1, r1l), (i0, i0l), (i1, i1l) = map(split, pair)
    x = grid([[r0, i0, r0l, i0l, r0, i0], [r1, i1, r1l, i1l, r1, i1]])
    y = jnp.dot(x, weight, preferred_element_type=jnp.float32)
    return y[:n, :n], y[n:, :n], y[:n, n:], y[n:, n:]


def times(pair, obj):
    (r0, r1, i0, i1), (a, b) = pair, obj
    return r0 * a - i0 * b, r1 * a - i1 * b, r0 * b + i0 * a, r1 * b + i1 * a


def times_conj(pair, obj):
    return times(pair, (obj[0], -obj[1]))


def positions(
    counts_ref, offsets_ref, obj_hbm, below_hbm, right_hbm, corner_hbm, probe_ref, amp_ref, lefts, rights,
    new_hbm, low_hbm, side_hbm, edge_hbm, sums_ref, ext, acc, window, waves, sems,
):
    depth, rows, cols = obj_hbm.shape[1:]
    n = probe_ref.shape[2]
    modes = probe_ref.shape[1]
    pairs = modes // 2
    slots = amp_ref.shape[0]
    parts = (
        (slice(0, rows), slice(0, cols)),
        (slice(rows, rows + n), slice(0, cols)),
        (slice(0, rows), slice(cols, cols + n)),
        (slice(rows, rows + n), slice(cols, cols + n)),
    )
    loads = [
        pltpu.make_async_copy(source, ext.at[:, :, r, c], sems.at[i])
        for i, (source, (r, c)) in enumerate(zip((obj_hbm, below_hbm, right_hbm, corner_hbm), parts))
    ]
    for copy in loads:
        copy.start()
    acc[...] = jnp.zeros_like(acc)
    sums_ref[...] = jnp.zeros_like(sums_ref)
    for copy in loads:
        copy.wait()
    tall = n + ROWS
    lane = lax.broadcasted_iota(jnp.int32, (tall, n), 1)

    def keep(level, p, pair):
        for c in range(2):
            for j in range(2):
                waves[level, c, 2 * p + j] = pair[2 * c + j]

    def kept(level, p):
        source = probe_ref if level == 0 else waves.at[level - 1]
        return tuple(source[c, 2 * p + j] for c in range(2) for j in range(2))

    @pl.loop(0, slots)
    def _(k):
        @pl.when(k < counts_ref[0, 0])
        def _():
            y = offsets_ref[0, 0, k, 0] % rows
            x = offsets_ref[0, 0, k, 1] % cols
            base = pl.multiple_of(x // n * n, n)
            step = x % n
            top = pl.multiple_of(y // ROWS * ROWS, ROWS)
            drop = y % ROWS
            for s in range(depth):
                for c in range(2):
                    near = ext[c, s, pl.ds(top, tall), pl.ds(base, n)]
                    far = ext[c, s, pl.ds(top, tall), pl.ds(base + n, n)]
                    turned = pltpu.roll(jnp.where(lane >= step, near, far), (n - step) % n, 1)
                    window[c, s] = pltpu.roll(turned, (tall - drop) % tall, 0)[:n]
            sums_ref[2 * modes] += window[0, 0] ** 2 + window[1, 0] ** 2

            state = [kept(0, p) for p in range(pairs)]
            for s in range(depth):
                obj = (window[0, s], window[1, s])
                state = [times(pair, obj) for pair in state]
                which = 0 if s < depth - 1 else 2
                state = [left_product(lefts[which], pair) for pair in state]
                state = [right_product(rights[which], pair) for pair in state]
                if s < depth - 1:
                    for p in range(pairs):
                        keep(s, p, state[p])
            intensity = sum(v * v for pair in state for v in pair)
            factor = 2.0 - 2.0 * amp_ref[k] / jnp.sqrt(intensity + 1.0)
            state = [tuple(v * factor for v in pair) for pair in state]
            for s in range(depth - 1, -1, -1):
                which = 1 if s < depth - 1 else 3
                state = [left_product(lefts[which], pair) for pair in state]
                state = [right_product(rights[which], pair) for pair in state]
                grads = [0.0, 0.0]
                for p in range(pairs):
                    w = kept(s, p)
                    g = state[p]
                    for j in range(2):
                        grads[0] += g[j] * w[j] + g[2 + j] * w[2 + j]
                        grads[1] += g[2 + j] * w[j] - g[j] * w[2 + j]
                for c in range(2):
                    moved = jnp.concatenate([grads[c] * STEP_OBJECT, jnp.zeros((ROWS, n), jnp.float32)], axis=0)
                    moved = pltpu.roll(pltpu.roll(moved, drop, 0), step, 1)
                    acc[c, s, pl.ds(top, tall), pl.ds(base, n)] += jnp.where(lane >= step, moved, 0.0)
                    acc[c, s, pl.ds(top, tall), pl.ds(base + n, n)] += jnp.where(lane >= step, 0.0, moved)
                obj = (window[0, s], window[1, s])
                state = [times_conj(pair, obj) for pair in state]
            for p in range(pairs):
                for c in range(2):
                    for j in range(2):
                        sums_ref[c * modes + 2 * p + j] += state[p][2 * c + j]

    r, c = parts[0]
    acc[:, :, r, c] = ext[:, :, r, c] - acc[:, :, r, c]
    stores = [
        pltpu.make_async_copy(acc.at[:, :, r, c], target, sems.at[i])
        for i, (target, (r, c)) in enumerate(zip((new_hbm, low_hbm, side_hbm, edge_hbm), parts))
    ]
    for copy in stores:
        copy.start()
    for copy in stores:
        copy.wait()


def shards(n_row, n_col, object_field, probe, amplitudes, offsets, counts):
    _, depth, rows, cols = object_field.shape
    modes, n = probe.shape[1:3]

    def shift(value, down, across, sign):
        pairs = []
        for a in range(n_row - down):
            for b in range(n_col - across):
                pair = ((a + down) * n_col + b + across, a * n_col + b)
                pairs.append(pair[::sign])
        return lax.ppermute(value, ("row", "col"), pairs)

    below = shift(object_field[:, :, :n, :], 1, 0, 1)
    right = shift(object_field[:, :, :, :n], 0, 1, 1)
    corner = shift(object_field[:, :, :n, :n], 1, 1, 1)
    lefts, rights = tables(n)
    f32 = jnp.float32
    vmem = pl.BlockSpec(memory_space=pltpu.VMEM)
    smem = pl.BlockSpec(memory_space=pltpu.SMEM)
    hbm = pl.BlockSpec(memory_space=pl.ANY)
    flops = amplitudes.shape[2] * depth * 4 * 2 * (modes * n) * (6 * n) * (2 * n)
    part, low, side, edge, sums = pl.pallas_call(
        positions,
        out_shape=(
            jax.ShapeDtypeStruct((2, depth, rows, cols), f32),
            jax.ShapeDtypeStruct((2, depth, n, cols), f32),
            jax.ShapeDtypeStruct((2, depth, rows, n), f32),
            jax.ShapeDtypeStruct((2, depth, n, n), f32),
            jax.ShapeDtypeStruct((2 * modes + 1, n, n), f32),
        ),
        in_specs=[smem, smem, hbm, hbm, hbm, hbm, vmem, vmem, vmem, vmem],
        out_specs=(hbm, hbm, hbm, hbm, vmem),
        scratch_shapes=[
            pltpu.VMEM((2, depth, rows + n, cols + n), f32),
            pltpu.VMEM((2, depth, rows + n, cols + n), f32),
            pltpu.VMEM((2, depth, n, n), f32),
            pltpu.VMEM((depth - 1, 2, modes, n, n), f32),
            pltpu.SemaphoreType.DMA((4,)),
        ],
        compiler_params=pltpu.CompilerParams(vmem_limit_bytes=48 * 2**20),
        cost_estimate=pl.CostEstimate(flops=flops, bytes_accessed=20 * 2**20, transcendentals=0),
        name="positions",
    )(counts, offsets, object_field, below, right, corner, probe, amplitudes[0, 0], jnp.asarray(lefts), jnp.asarray(rights))
    totals = lax.psum(sums, ("row", "col"))
    low = shift(low, 1, 0, -1)
    side = shift(side, 0, 1, -1)
    edge = shift(edge, 1, 1, -1)

    def widen(value):
        gaps = [(0, 0, 0), (0, 0, 0), (0, rows - value.shape[2], 0), (0, cols - value.shape[3], 0)]
        return lax.pad(value, jnp.zeros((), f32), gaps)

    new_object = part - widen(low) - widen(side) - widen(edge)
    grad_total = totals[: 2 * modes].reshape(probe.shape)
    new_probe = probe - STEP_PROBE * grad_total / (totals[2 * modes] + 1.0)
    return (new_object, new_probe)


def solution(mesh):
    return jax.shard_map(
        partial(shards, mesh.shape["row"], mesh.shape["col"]),
        mesh=mesh,
        in_specs=(
            P(None, None, "row", "col"),
            P(),
            P("row", "col", None, None, None),
            P("row", "col", None, None),
            P("row", "col"),
        ),
        out_specs=(P(None, None, "row", "col"), P()),
        check_vma=False,
    )
```

time: 562 us -> 235 us (0.42)
  matrix products: 233 us -> 0 us
  local copies, waits for them, and re-layouts: 86.9 us -> 7.48 us
  Pallas kernels: 0 us -> 31 us
  between operations: 35 us -> 14.8 us
  waiting for transfers between devices: 171 us -> 154 us
  other arithmetic: 19.2 us -> 6.25 us
  starting transfers between devices: 11.5 us -> 21.4 us
    dot_general x112 -> x0, matrix products: 233 us -> none  [the longest x14 33.5 us: product_left(): contract('jk,mkl->mjl', table_real, field_real)]
    dynamic_update_slice x5 -> x0, local copies, waits for them, and re-layouts: 37.9 us -> none  [shards(): lax.dynamic_update_slice(grad_ext, previous + grad_windows[slot_index], s...]
    pallas_call x0 -> x1, Pallas kernels: none -> 31 us  [shards(): pl.pallas_call(positions, out_shape=(jax.ShapeDtypeStruct((2, depth, rows...]
    gather x15 -> x0, local copies, waits for them, and re-layouts: 20.9 us -> none
    ppermute x4 -> x6, waiting for transfers between devices: 42.7 us -> 32.6 us  [shift(): return lax.ppermute(value, ('row', 'col'), pairs)]
    ppermute x4 -> x6, starting transfers between devices: 11.5 us -> 21.4 us  [shift(): return lax.ppermute(value, ('row', 'col'), pairs)]
    mul x7 -> x0, local copies, waits for them, and re-layouts: 9.47 us -> none  [the longest x5 7.5 us: position_loss(): wave_real * object_real - wave_imag * object_imag]
    psum x1, waiting for transfers between devices: 129 us -> 121 us  [shards(): totals = lax.psum(sums, ('row', 'col'))]
  transfers between devices with their start and end apart: 5 -> 7, of which waited for: 3 -> 2; matrix products, arithmetic and copies ran while one was open for 2% -> 2% of each run, Pallas kernels for 0% -> 0%
where the time goes in v1:
time: 235 us
  waiting for transfers between devices  154 us (66%)
  Pallas kernels  31 us (13%)
  starting transfers between devices  21.4 us (9%)
  between operations  14.8 us (6%)
  local copies, waits for them, and re-layouts  7.48 us (3%)
  other arithmetic  6.25 us (3%)
    psum x1, waiting for transfers between devices, shards(): totals = lax.psum(sums, ('row', 'col'))  121 us
    ppermute x6, waiting for transfers between devices, shift(): return lax.ppermute(value, ('row', 'col'), pairs)  32.6 us
    pallas_call x1, Pallas kernels, shards(): pl.pallas_call(positions, out_shape=(jax.ShapeDtypeStruct((2, depth, rows...  31 us
    ppermute x6, starting transfers between devices, shift(): return lax.ppermute(value, ('row', 'col'), pairs)  21.4 us
  transfers between devices with their start and end apart: 7, of which 2 were waited for; matrix products, arithmetic and copies ran while one was open for 2% of the time, Pallas kernels for 0%

profile of v1, /device:TPU:1, one launch (start us, length us, event | category | flops | bytes accessed | tf_op | source)
XLA Modules:
  0.0 234.8 jit_solution(4897479864134642257)
XLA Ops:
  7.2 0.0 all-reduce.5.cloned.1.call-start
  7.2 0.0 copy-start.6
  7.2 1.4 slice.15
  8.7 0.0 copy-start.8
  8.7 0.0 copy-start
  8.7 0.0 copy-start.5
  8.7 1.4 collective-permute-start
  10.2 1.1 slice.16
  11.2 2.0 collective-permute-start.1
  13.2 0.8 slice.17
  14.0 1.3 collective-permute-start.2
  15.9 0.1 copy.9.offsets_ref
  16.0 32.6 %collective-permute-done.2.corner_hbm = f32[2,4,128,128]{3,2,1,0:T(8,128)S(1)} collective-permute-done((f32[2,4,128,128]{3,2,1,0:T(8,128)}, f32[2,4,128,128]{3,2,1,0:T(8,128)S(1)}, u32[]{:S(2)}, u32[]{:S(2)}) %collective-permute-start.2) | collective-permute-done | bytes 524320 | tf_op jit(solution)/shard_map/ppermute | solution.py:188
  48.6 0.8 copy-done.3
  49.4 0.0 collective-permute-done.below_hbm
  49.4 1.0 copy-done.1
  50.4 0.0 collective-permute-done.1.right_hbm
  50.4 1.2 copy-done.2
  51.6 1.0 copy-done.4
  52.7 31.0 %positions.1 = (f32[2,4,256,256]{3,2,1,0:T(8,128)}, f32[2,4,128,256]{3,2,1,0:T(8,128)S(1)}, f32[2,4,256,128]{3,2,1,0:T(8,128)S(1)}, f32[2,4,128,128]{3,2,1,0:T(8,128)S(1)}, f32[9,128,128]{2,1,0:T(8,128)}) custom-call(s32[1,1]{1,0:T(1,128)S(6)} %copy.11.counts_ref, s32[1,1,5,2]{3,2,1,0:T(8,128)S(1)} %copy.9.offsets_ref, f32[2,4,256,256]{3,2,1,0:T(8,128)} %obj_hbm.1, ...), custom_call_target="tpu_custom_call" | custom-call | flops 16106127360 | bytes 20971520 | tf_op jit(solution)/shard_map/positions/pallas_call | solution.py:199
  83.7 2.3 collective-permute-start.3
  86.0 7.8 %collective-permute-start.4 = (f32[2,4,256,128]{3,2,1,0:T(8,128)S(1)}, f32[2,4,256,128]{3,2,1,0:T(8,128)}, u32[]{:S(2)}, u32[]{:S(2)}) collective-permute-start(f32[2,4,256,128]{3,2,1,0:T(8,128)S(1)} %get-tuple-element.9), channel_id=1, source_target_pairs={{0,1},{1,2},{2,3},{3,4},{4,5},{5,6},{6,7},{8,9},{9,10},{10,11},{11... | collective-permute-start | bytes 3145736 | tf_op jit(solution)/shard_map/ppermute | solution.py:188
  93.8 0.0 all-reduce.5.cloned.1.call-update
  93.8 6.6 %collective-permute-start.5 = (f32[2,4,128,128]{3,2,1,0:T(8,128)S(1)}, f32[2,4,128,128]{3,2,1,0:T(8,128)}, u32[]{:S(2)}, u32[]{:S(2)}) collective-permute-start(f32[2,4,128,128]{3,2,1,0:T(8,128)S(1)} %get-tuple-element.10), channel_id=1, source_target_pairs={{0,9},{1,10},{2,11},{3,12},{4,13},{5,14},{6,15},{8,17},{9,18},{10,... | collective-permute-start | bytes 1572872 | tf_op jit(solution)/shard_map/ppermute | solution.py:188
  100.4 121.3 %all-reduce.5.cloned.1.call-done = f32[9,128,128]{2,1,0:T(8,128)} async-done(((f32[9,128,128]{2,1,0:T(8,128)}), f32[9,128,128]{2,1,0:T(8,128)}) %all-reduce.5.cloned.1.call-update) | async-done | bytes 589840 | tf_op jit(solution)/shard_map/psum | solution.py:221
  221.7 1.0 fusion
  222.7 1.1 slice_multiply_fusion
  223.8 0.9 divide_subtract_fusion
  224.6 0.0 collective-permute-done.5
  224.6 0.0 collective-permute-done.3
  224.7 0.0 collective-permute-done.4
  224.7 3.3 %pad_subtract_fusion = f32[2,4,256,256]{3,2,1,0:T(8,128)} fusion(f32[2,4,128,128]{3,2,1,0:T(8,128)} %collective-permute-done.5, f32[2,4,256,128]{3,2,1,0:T(8,128)} %collective-permute-done.4, f32[2,4,256,256]{3,2,1,0:T(8,128)S(1)} %copy-done.7, f32[2,4,128,256]{3,2,1,0:T(8,128)} %collective-permute-done.3), kind=kLoop, calls=%fused_computation | loop fusion | flops 1572864 | bytes 6815744 | tf_op jit(solution)/shard_map/sub | solution.py:230
  (10 shorter events, 0.0 us)
Async XLA Ops:
  7.2 214.5 %all-reduce.5.cloned.1.call-start = ((), (), s32[]{:S(2)}) async-start(), calls=%async_computation | async-start | bytes 1179648 | tf_op jit(solution)/shard_map/psum | solution.py:221
  7.2 2.9 %copy-start.6 = (f32[2,4,256,256]{3,2,1,0:T(8,128)S(1)}, f32[2,4,256,256]{3,2,1,0:T(8,128)}, u32[]{:S(2)}) copy-start(f32[2,4,256,256]{3,2,1,0:T(8,128)} %obj_hbm.1) | copy-start | bytes 6291460
  8.7 7.3 %copy-start.8 = (s32[1,1,5,2]{2,3,1,0:T(2,128)S(1)}, s32[1,1,5,2]{2,3,1,0:T(2,128)}, u32[]{:S(2)}) copy-start(s32[1,1,5,2]{2,3,1,0:T(2,128)} %param.10) | copy-start | bytes 124
  8.7 41.7 %copy-start = (f32[2,4,128,128]{3,2,1,0:T(8,128)S(1)}, f32[2,4,128,128]{3,2,1,0:T(8,128)}, u32[]{:S(2)}) copy-start(f32[2,4,128,128]{3,2,1,0:T(8,128)} %probe_ref.1) | copy-start | bytes 1572868
  8.7 41.7 %copy-start.5 = (f32[1,1,5,128,128]{4,3,2,1,0:T(8,128)S(1)}, f32[1,1,5,128,128]{4,3,2,1,0:T(8,128)}, u32[]{:S(2)}) copy-start(f32[1,1,5,128,128]{4,3,2,1,0:T(8,128)} %param.9) | copy-start | bytes 983044
  8.7 40.7 %collective-permute-start = (f32[2,4,128,256]{3,2,1,0:T(8,128)S(1)}, f32[2,4,128,256]{3,2,1,0:T(8,128)S(1)}, u32[]{:S(2)}, u32[]{:S(2)}) collective-permute-start(f32[2,4,128,256]{3,2,1,0:T(8,128)S(1)} %slice.15), channel_id=1, source_target_pairs={{8,0},{9,1},{10,2},{11,3},{12,4},{13,5},{14,6},{15,7},{16,8},{17,9... | collective-permute-start | bytes 3145736 | tf_op jit(solution)/shard_map/ppermute | solution.py:188
  11.2 39.2 %collective-permute-start.1 = (f32[2,4,256,128]{3,2,1,0:T(8,128)}, f32[2,4,256,128]{3,2,1,0:T(8,128)}, u32[]{:S(2)}, u32[]{:S(2)}) collective-permute-start(f32[2,4,256,128]{3,2,1,0:T(8,128)} %slice.16), channel_id=1, source_target_pairs={{1,0},{2,1},{3,2},{4,3},{5,4},{6,5},{7,6},{9,8},{10,9},{11,10},{12... | collective-permute-start | bytes 3145736 | tf_op jit(solution)/shard_map/ppermute | solution.py:188
  14.0 34.6 %collective-permute-start.2 = (f32[2,4,128,128]{3,2,1,0:T(8,128)}, f32[2,4,128,128]{3,2,1,0:T(8,128)S(1)}, u32[]{:S(2)}, u32[]{:S(2)}) collective-permute-start(f32[2,4,128,128]{3,2,1,0:T(8,128)} %slice.17), channel_id=1, source_target_pairs={{9,0},{10,1},{11,2},{12,3},{13,4},{14,5},{15,6},{17,8},{18,9},{19,... | collective-permute-start | bytes 1572872 | tf_op jit(solution)/shard_map/ppermute | solution.py:188
  48.6 0.8 copy-start.3
  49.4 1.0 copy-start.1
  50.4 1.2 copy-start.2
  51.6 1.0 copy-start.4
  83.7 141.0 %collective-permute-start.3 = (f32[2,4,128,256]{3,2,1,0:T(8,128)S(1)}, f32[2,4,128,256]{3,2,1,0:T(8,128)}, u32[]{:S(2)}, u32[]{:S(2)}) collective-permute-start(f32[2,4,128,256]{3,2,1,0:T(8,128)S(1)} %get-tuple-element.8), channel_id=1, source_target_pairs={{0,8},{1,9},{2,10},{3,11},{4,12},{5,13},{6,14},{7,15},{8,16},{9,17... | collective-permute-start | bytes 3145736 | tf_op jit(solution)/shard_map/ppermute | solution.py:188
  86.0 138.7 %collective-permute-start.4 = (f32[2,4,256,128]{3,2,1,0:T(8,128)S(1)}, f32[2,4,256,128]{3,2,1,0:T(8,128)}, u32[]{:S(2)}, u32[]{:S(2)}) collective-permute-start(f32[2,4,256,128]{3,2,1,0:T(8,128)S(1)} %get-tuple-element.9), channel_id=1, source_target_pairs={{0,1},{1,2},{2,3},{3,4},{4,5},{5,6},{6,7},{8,9},{9,10},{10,11},{11... | collective-permute-start | bytes 3145736 | tf_op jit(solution)/shard_map/ppermute | solution.py:188
  93.8 130.8 %collective-permute-start.5 = (f32[2,4,128,128]{3,2,1,0:T(8,128)S(1)}, f32[2,4,128,128]{3,2,1,0:T(8,128)}, u32[]{:S(2)}, u32[]{:S(2)}) collective-permute-start(f32[2,4,128,128]{3,2,1,0:T(8,128)S(1)} %get-tuple-element.10), channel_id=1, source_target_pairs={{0,9},{1,10},{2,11},{3,12},{4,13},{5,14},{6,15},{8,17},{9,18},{10,... | collective-permute-start | bytes 1572872 | tf_op jit(solution)/shard_map/ppermute | solution.py:188
  221.7 3.0 %copy-start.7 = (f32[2,4,256,256]{3,2,1,0:T(8,128)S(1)}, f32[2,4,256,256]{3,2,1,0:T(8,128)}, u32[]{:S(2)}) copy-start(f32[2,4,256,256]{3,2,1,0:T(8,128)} %get-tuple-element.7) | copy-start | bytes 6291460
Sparse Core Ops, SparseCore 0:
  93.9 127.7 all-reduce.4

commit v2 on v1

--- a/solution.py
+++ b/solution.py
@@ -125,7 +125,7 @@
                     far = ext[c, s, pl.ds(top, tall), pl.ds(base + n, n)]
                     turned = pltpu.roll(jnp.where(lane >= step, near, far), (n - step) % n, 1)
                     window[c, s] = pltpu.roll(turned, (tall - drop) % tall, 0)[:n]
-            sums_ref[2 * modes] += window[0, 0] ** 2 + window[1, 0] ** 2
+            sums_ref[pl.ds(2 * modes * n, n)] += window[0, 0] ** 2 + window[1, 0] ** 2
 
             state = [kept(0, p) for p in range(pairs)]
             for s in range(depth):
@@ -161,7 +161,7 @@
             for p in range(pairs):
                 for c in range(2):
                     for j in range(2):
-                        sums_ref[c * modes + 2 * p + j] += state[p][2 * c + j]
+                        sums_ref[pl.ds((c * modes + 2 * p + j) * n, n)] += state[p][2 * c + j]
 
     r, c = parts[0]
     acc[:, :, r, c] = ext[:, :, r, c] - acc[:, :, r, c]
@@ -175,35 +175,249 @@
         copy.wait()
 
 
+def remote(source, target, send, recv, device):
+    return pltpu.make_async_remote_copy(
+        src_ref=source, dst_ref=target, send_sem=send, recv_sem=recv,
+        device_id=device, device_id_type=pl.DeviceIdType.MESH,
+    )
+
+
+def signal(device):
+    pl.semaphore_signal(
+        pltpu.get_barrier_semaphore(), inc=1, device_id=device, device_id_type=pl.DeviceIdType.MESH
+    )
+
+
+def gather(n_row, n_col, obj, below, right, corner, send, recv):
+    a, b = lax.axis_index("row"), lax.axis_index("col")
+    depth, n = below.shape[1:3]
+    has_up, has_down, has_left, has_right = a > 0, a < n_row - 1, b > 0, b < n_col - 1
+    up, left = (a - 1, b), (a, b - 1)
+    barrier = pltpu.get_barrier_semaphore()
+
+    @pl.when(has_down)
+    def _():
+        signal((a + 1, b))
+
+    @pl.when(has_right)
+    def _():
+        signal((a, b + 1))
+
+    rows = [
+        remote(obj.at[:, s, pl.ds(0, n), :], below.at[:, s], send.at[0, s], recv.at[0, s], up) for s in range(depth)
+    ]
+    side = remote(obj.at[:, :, :, pl.ds(0, n)], right, send.at[1, 0], recv.at[1, 0], left)
+    edges = [
+        remote(below.at[:, s, :, pl.ds(0, n)], corner.at[:, s], send.at[2, s], recv.at[2, s], left)
+        for s in range(depth)
+    ]
+
+    @pl.when(has_up & has_left)
+    def _():
+        pl.semaphore_wait(barrier, 2)
+
+    @pl.when(has_up != has_left)
+    def _():
+        pl.semaphore_wait(barrier, 1)
+
+    @pl.when(has_up)
+    def _():
+        for copy in rows:
+            copy.start()
+
+    @pl.when(has_left)
+    def _():
+        side.start()
+
+    for s in range(depth):
+
+        @pl.when(has_down)
+        def _():
+            rows[s].wait_recv()
+
+        @pl.when(has_down & has_left)
+        def _():
+            edges[s].start()
+
+    @pl.when(has_right)
+    def _():
+        side.wait_recv()
+
+    @pl.when(has_down & has_right)
+    def _():
+        for copy in edges:
+            copy.wait_recv()
+
+    @pl.when(has_up)
+    def _():
+        for copy in rows:
+            copy.wait_send()
+
+    @pl.when(has_left)
+    def _():
+        side.wait_send()
+
+    @pl.when(has_down & has_left)
+    def _():
+        for copy in edges:
+            copy.wait_send()
+
+
+def finish(
+    n_row, n_col, part, low, side, edge, sums, probe, new_object, new_probe,
+    low_out, low_in, side_in, edge_in, first, middle, second, total,
+    send, recv, col_send, col_recv, row_send, row_recv,
+):
+    a, b = lax.axis_index("row"), lax.axis_index("col")
+    depth, n = low.shape[1:3]
+    modes = probe.shape[1]
+    big = middle.shape[0]
+    small = big // n_row
+    has_up, has_down, has_left, has_right = a > 0, a < n_row - 1, b > 0, b < n_col - 1
+    col_peers = [lax.rem(b + i, n_col) for i in range(1, n_col)]
+    row_peers = [lax.rem(a + i, n_row) for i in range(1, n_row)]
+    barrier = pltpu.get_barrier_semaphore()
+    for peer in col_peers:
+        signal((a, peer))
+    for peer in row_peers:
+        signal((peer, b))
+    pl.semaphore_wait(barrier, n_col - 1 + n_row - 1)
+
+    def chunk(ref, index, size):
+        return ref.at[pl.ds(pl.multiple_of(index * size, ROWS), size)]
+
+    scatter_col = [
+        remote(chunk(sums, peer, big), first.at[i], col_send.at[0, i], col_recv.at[0, i], (a, peer))
+        for i, peer in enumerate(col_peers)
+    ]
+    for copy in scatter_col:
+        copy.start()
+    right, down = (a, b + 1), (a + 1, b)
+    edges = [remote(edge.at[:, s], edge_in.at[:, s], send.at[0, s], recv.at[0, s], right) for s in range(depth)]
+    sides = remote(side, side_in, send.at[1, 0], recv.at[1, 0], right)
+    lows = [remote(low_out.at[:, s], low_in.at[:, s], send.at[2, s], recv.at[2, s], down) for s in range(depth)]
+
+    @pl.when(has_down & has_right)
+    def _():
+        for copy in edges:
+            copy.start()
+
+    @pl.when(has_right)
+    def _():
+        sides.start()
+
+    for s in range(depth):
+        low_out[:, s] = low[:, s]
+
+        @pl.when(has_down & has_left)
+        def _():
+            edges[s].wait_recv()
+            low_out[:, s, :, :n] += edge_in[:, s]
+
+        @pl.when(has_down)
+        def _():
+            lows[s].start()
+
+    for copy in scatter_col:
+        copy.wait()
+    mine = chunk(sums, b, big)[...]
+    for i in range(n_col - 1):
+        mine += first[i]
+    middle[...] = mine
+    scatter_row = [
+        remote(chunk(middle, peer, small), second.at[i], row_send.at[0, i], row_recv.at[0, i], (peer, b))
+        for i, peer in enumerate(row_peers)
+    ]
+    for copy in scatter_row:
+        copy.start()
+    for copy in scatter_row:
+        copy.wait()
+    mine = chunk(middle, a, small)[...]
+    for i in range(n_row - 1):
+        mine += second[i]
+    own = chunk(total, b * n_row + a, small)
+    own[...] = mine
+    gather_row = [
+        remote(own, own, row_send.at[1, i], row_recv.at[1, i], (peer, b)) for i, peer in enumerate(row_peers)
+    ]
+    for copy in gather_row:
+        copy.start()
+    for copy in gather_row:
+        copy.wait()
+    group = chunk(total, b, big)
+    gather_col = [
+        remote(group, group, col_send.at[1, i], col_recv.at[1, i], (a, peer)) for i, peer in enumerate(col_peers)
+    ]
+    for copy in gather_col:
+        copy.start()
+    new_object[...] = part[...]
+
+    @pl.when(has_left)
+    def _():
+        sides.wait_recv()
+        new_object[:, :, :, :n] -= side_in[...]
+
+    for s in range(depth):
+
+        @pl.when(has_up)
+        def _():
+            lows[s].wait_recv()
+            new_object[:, s, :n] -= low_in[:, s]
+
+    for copy in gather_col:
+        copy.wait()
+    scale = STEP_PROBE / (total[pl.ds(2 * modes * n, n)] + 1.0)
+    for c in range(2):
+        for m in range(modes):
+            new_probe[c, m] = probe[c, m] - total[pl.ds((c * modes + m) * n, n)] * scale
+
+    @pl.when(has_down & has_right)
+    def _():
+        for copy in edges:
+            copy.wait_send()
+
+    @pl.when(has_right)
+    def _():
+        sides.wait_send()
+
+    @pl.when(has_down)
+    def _():
+        for copy in lows:
+            copy.wait_send()
+
+
 def shards(n_row, n_col, object_field, probe, amplitudes, offsets, counts):
     _, depth, rows, cols = object_field.shape
     modes, n = probe.shape[1:3]
-
-    def shift(value, down, across, sign):
-        pairs = []
-        for a in range(n_row - down):
-            for b in range(n_col - across):
-                pair = ((a + down) * n_col + b + across, a * n_col + b)
-                pairs.append(pair[::sign])
-        return lax.ppermute(value, ("row", "col"), pairs)
-
-    below = shift(object_field[:, :, :n, :], 1, 0, 1)
-    right = shift(object_field[:, :, :, :n], 0, 1, 1)
-    corner = shift(object_field[:, :, :n, :n], 1, 1, 1)
-    lefts, rights = tables(n)
     f32 = jnp.float32
     vmem = pl.BlockSpec(memory_space=pltpu.VMEM)
     smem = pl.BlockSpec(memory_space=pltpu.SMEM)
     hbm = pl.BlockSpec(memory_space=pl.ANY)
+    rims = (
+        jax.ShapeDtypeStruct((2, depth, n, cols), f32),
+        jax.ShapeDtypeStruct((2, depth, rows, n), f32),
+        jax.ShapeDtypeStruct((2, depth, n, n), f32),
+    )
+    dma = pltpu.SemaphoreType.DMA
+    below, right, corner = pl.pallas_call(
+        partial(gather, n_row, n_col),
+        out_shape=rims,
+        in_specs=[hbm],
+        out_specs=(hbm, hbm, hbm),
+        scratch_shapes=[dma((3, depth)), dma((3, depth))],
+        compiler_params=pltpu.CompilerParams(collective_id=0, has_side_effects=True),
+        name="gather",
+    )(object_field)
+    lefts, rights = tables(n)
     flops = amplitudes.shape[2] * depth * 4 * 2 * (modes * n) * (6 * n) * (2 * n)
+    devices = n_row * n_col
+    small = -(-(2 * modes + 1) * n // (devices * ROWS)) * ROWS
     part, low, side, edge, sums = pl.pallas_call(
         positions,
         out_shape=(
             jax.ShapeDtypeStruct((2, depth, rows, cols), f32),
-            jax.ShapeDtypeStruct((2, depth, n, cols), f32),
-            jax.ShapeDtypeStruct((2, depth, rows, n), f32),
-            jax.ShapeDtypeStruct((2, depth, n, n), f32),
-            jax.ShapeDtypeStruct((2 * modes + 1, n, n), f32),
+            *rims,
+            jax.ShapeDtypeStruct((devices * small, n), f32),
         ),
         in_specs=[smem, smem, hbm, hbm, hbm, hbm, vmem, vmem, vmem, vmem],
         out_specs=(hbm, hbm, hbm, hbm, vmem),
@@ -212,25 +426,41 @@
             pltpu.VMEM((2, depth, rows + n, cols + n), f32),
             pltpu.VMEM((2, depth, n, n), f32),
             pltpu.VMEM((depth - 1, 2, modes, n, n), f32),
-            pltpu.SemaphoreType.DMA((4,)),
+            dma((4,)),
         ],
-        compiler_params=pltpu.CompilerParams(vmem_limit_bytes=48 * 2**20),
+        compiler_params=pltpu.CompilerParams(vmem_limit_bytes=56 * 2**20),
         cost_estimate=pl.CostEstimate(flops=flops, bytes_accessed=20 * 2**20, transcendentals=0),
         name="positions",
     )(counts, offsets, object_field, below, right, corner, probe, amplitudes[0, 0], jnp.asarray(lefts), jnp.asarray(rights))
-    totals = lax.psum(sums, ("row", "col"))
-    low = shift(low, 1, 0, -1)
-    side = shift(side, 0, 1, -1)
-    edge = shift(edge, 1, 1, -1)
-
-    def widen(value):
-        gaps = [(0, 0, 0), (0, 0, 0), (0, rows - value.shape[2], 0), (0, cols - value.shape[3], 0)]
-        return lax.pad(value, jnp.zeros((), f32), gaps)
-
-    new_object = part - widen(low) - widen(side) - widen(edge)
-    grad_total = totals[: 2 * modes].reshape(probe.shape)
-    new_probe = probe - STEP_PROBE * grad_total / (totals[2 * modes] + 1.0)
-    return (new_object, new_probe)
+    return pl.pallas_call(
+        partial(finish, n_row, n_col),
+        out_shape=(
+            jax.ShapeDtypeStruct(object_field.shape, f32),
+            jax.ShapeDtypeStruct(probe.shape, f32),
+        ),
+        in_specs=[vmem] * 6,
+        out_specs=(vmem, vmem),
+        scratch_shapes=[
+            pltpu.VMEM(rims[0].shape, f32),
+            pltpu.VMEM(rims[0].shape, f32),
+            pltpu.VMEM(rims[1].shape, f32),
+            pltpu.VMEM(rims[2].shape, f32),
+            pltpu.VMEM((n_col - 1, n_row * small, n), f32),
+            pltpu.VMEM((n_row * small, n), f32),
+            pltpu.VMEM((n_row - 1, small, n), f32),
+            pltpu.VMEM((devices * small, n), f32),
+            dma((3, depth)),
+            dma((3, depth)),
+            dma((2, n_col - 1)),
+            dma((2, n_col - 1)),
+            dma((2, n_row - 1)),
+            dma((2, n_row - 1)),
+        ],
+        compiler_params=pltpu.CompilerParams(
+            collective_id=1, has_side_effects=True, vmem_limit_bytes=40 * 2**20
+        ),
+        name="finish",
+    )(part, low, side, edge, sums, probe)
 
 
 def solution(mesh):

time: 235 us -> 122 us (0.52)
  waiting for transfers between devices: 154 us -> 0 us
  Pallas kernels: 31 us -> 111 us
  starting transfers between devices: 21.4 us -> 0 us
  between operations: 14.8 us -> 1.33 us
  other arithmetic: 6.25 us -> 0 us
    psum x1 -> x0, waiting for transfers between devices: 121 us -> none  [shards(): totals = lax.psum(sums, ('row', 'col'))]
    pallas_call x0 -> x2, Pallas kernels: none -> 96.7 us  [the longest x1 65.2 us: shards(): pl.pallas_call(partial(finish, n_row, n_col), out_shape=(jax.ShapeDtypeSt...]
    ppermute x6 -> x0, waiting for transfers between devices: 32.6 us -> none  [shift(): return lax.ppermute(value, ('row', 'col'), pairs)]
    ppermute x6 -> x0, starting transfers between devices: 21.4 us -> none  [shift(): return lax.ppermute(value, ('row', 'col'), pairs)]
    pallas_call x1, Pallas kernels: 31 us -> 14 us  [shards(): pl.pallas_call(positions, out_shape=(jax.ShapeDtypeStruct((2, depth, rows...]
    unnamed x19 -> x15, local copies, waits for them, and re-layouts: 4.14 us -> 9.63 us
    sub x2 -> x0, other arithmetic: 4.17 us -> none  [the longest x1 3.32 us: shards(): new_object = part - widen(low) - widen(side) - widen(edge)]
    slice x3 -> x0, local copies, waits for them, and re-layouts: 3.33 us -> none  [the longest x1 1.45 us: shards(): below = shift(object_field[:, :, :n, :], 1, 0, 1)]
  transfers between devices with their start and end apart: 7 -> 0, of which waited for: 2 -> 0; matrix products, arithmetic and copies ran while one was open for 2% -> 0% of each run, Pallas kernels for 0% -> 0%
where the time goes in v2:
time: 122 us
  Pallas kernels  111 us (91%)
  local copies, waits for them, and re-layouts  9.63 us (8%)
  between operations  1.33 us (1%)
    pallas_call x1, Pallas kernels, shards(): pl.pallas_call(partial(finish, n_row, n_col), out_shape=(jax.ShapeDtypeSt...  65.2 us
    pallas_call x1, Pallas kernels, shards(): pl.pallas_call(partial(gather, n_row, n_col), out_shape=rims, in_specs=[h...  31.5 us
    pallas_call x1, Pallas kernels, shards(): pl.pallas_call(positions, out_shape=(jax.ShapeDtypeStruct((2, depth, rows...  14 us
    unnamed x15, local copies, waits for them, and re-layouts  9.63 us

profile of v2, /device:TPU:1, one launch (start us, length us, event | category | flops | bytes accessed | tf_op | source)
XLA Modules:
  0.0 121.7 jit_solution(2853748105753639370)
XLA Ops:
  1.3 1.3 %copy.9.offsets_ref = s32[1,1,5,2]{3,2,1,0:T(8,128)} copy(s32[1,1,5,2]{2,3,1,0:T(2,128)} %param.10) | data formatting | bytes 80 | tf_op args[3]
  2.6 31.5 %gather.1 = (f32[2,4,128,256]{3,2,1,0:T(8,128)}, f32[2,4,256,128]{3,2,1,0:T(8,128)}, f32[2,4,128,128]{3,2,1,0:T(8,128)}) custom-call(f32[2,4,256,256]{3,2,1,0:T(8,128)} %obj_hbm.1), custom_call_target="tpu_custom_call" | custom-call | tf_op jit(solution)/shard_map/gather/pallas_call | solution.py:402
  34.1 0.0 copy-start.4
  34.1 14.0 %positions.1 = (f32[2,4,256,256]{3,2,1,0:T(8,128)}, f32[2,4,128,256]{3,2,1,0:T(8,128)}, f32[2,4,256,128]{3,2,1,0:T(8,128)}, f32[2,4,128,128]{3,2,1,0:T(8,128)}, f32[1280,128]{1,0:T(8,128)}) custom-call(s32[1,1]{1,0:T(1,128)S(6)} %copy.12.counts_ref, s32[1,1,5,2]{3,2,1,0:T(8,128)} %copy.9.offsets_ref, f32[2,4,256,256]{3,2,1,0:T(8,128)} %obj_hbm.1, ...), custom_call_target="tpu_custom_call" | custom-call | flops 16106127360 | bytes 20971520 | tf_op jit(solution)/shard_map/positions/pallas_call | solution.py:415
  48.2 0.0 copy-done.4
  48.2 0.0 copy-start
  48.2 1.6 %copy-done = f32[2,4,256,256]{3,2,1,0:T(8,128)S(1)} copy-done((f32[2,4,256,256]{3,2,1,0:T(8,128)S(1)}, f32[2,4,256,256]{3,2,1,0:T(8,128)}, u32[]{:S(2)}) %copy-start) | copy-done | bytes 2097176
  49.8 0.0 copy-start.1
  49.8 1.2 %copy-done.1 = f32[2,4,128,256]{3,2,1,0:T(8,128)S(1)} copy-done((f32[2,4,128,256]{3,2,1,0:T(8,128)S(1)}, f32[2,4,128,256]{3,2,1,0:T(8,128)}, u32[]{:S(2)}) %copy-start.1) | copy-done | bytes 1048600
  51.0 0.0 copy-start.2
  51.0 1.2 %copy-done.2 = f32[2,4,256,128]{3,2,1,0:T(8,128)S(1)} copy-done((f32[2,4,256,128]{3,2,1,0:T(8,128)S(1)}, f32[2,4,256,128]{3,2,1,0:T(8,128)}, u32[]{:S(2)}) %copy-start.2) | copy-done | bytes 1048600
  52.2 0.0 copy-start.3
  52.2 1.1 copy-done.3
  53.3 0.0 copy-start.5
  53.3 1.0 copy-done.5
  54.4 65.2 %finish.1 = (f32[2,4,256,256]{3,2,1,0:T(8,128)S(1)}, f32[2,4,128,128]{3,2,1,0:T(8,128)S(1)}) custom-call(f32[2,4,256,256]{3,2,1,0:T(8,128)S(1)} %copy-done, f32[2,4,128,256]{3,2,1,0:T(8,128)S(1)} %copy-done.1, f32[2,4,256,128]{3,2,1,0:T(8,128)S(1)} %copy-done.2, f32[2,4,128,128]{3,2,1,0:T(8,128)S(1)} %copy-done.5, f32[1280,128]{1,0:T(8,128)S(1)} %copy-done.3, ...), custom_call_target="tpu_custom_call" | custom-call | tf_op jit(solution)/shard_map/finish/pallas_call | solution.py:435
  119.6 1.3 %copy.13 = f32[2,4,256,256]{3,2,1,0:T(8,128)} copy(f32[2,4,256,256]{3,2,1,0:T(8,128)S(1)} %get-tuple-element.20) | data formatting | bytes 4194304
  120.9 0.8 copy.14
Async XLA Ops:
  34.1 14.0 %copy-start.4 = (f32[2,4,128,128]{3,2,1,0:T(8,128)S(1)}, f32[2,4,128,128]{3,2,1,0:T(8,128)}, u32[]{:S(2)}) copy-start(f32[2,4,128,128]{3,2,1,0:T(8,128)} %probe.1) | copy-start | bytes 1572868
  48.2 1.6 %copy-start = (f32[2,4,256,256]{3,2,1,0:T(8,128)S(1)}, f32[2,4,256,256]{3,2,1,0:T(8,128)}, u32[]{:S(2)}) copy-start(f32[2,4,256,256]{3,2,1,0:T(8,128)} %get-tuple-element.13.part) | copy-start | bytes 6291460
  49.8 1.2 %copy-start.1 = (f32[2,4,128,256]{3,2,1,0:T(8,128)S(1)}, f32[2,4,128,256]{3,2,1,0:T(8,128)}, u32[]{:S(2)}) copy-start(f32[2,4,128,256]{3,2,1,0:T(8,128)} %get-tuple-element.14.low) | copy-start | bytes 3145732
  51.0 1.2 %copy-start.2 = (f32[2,4,256,128]{3,2,1,0:T(8,128)S(1)}, f32[2,4,256,128]{3,2,1,0:T(8,128)}, u32[]{:S(2)}) copy-start(f32[2,4,256,128]{3,2,1,0:T(8,128)} %get-tuple-element.15.side) | copy-start | bytes 3145732
  52.2 1.1 copy-start.3
  53.3 1.0 copy-start.5

commit v3 on v1

v3 whole, which is shorter than its diff:
```python
from functools import partial
import math

import jax
import jax.numpy as jnp
import ml_dtypes
import numpy as np
from jax import lax
from jax.experimental import pallas as pl
from jax.experimental.pallas import tpu as pltpu
from jax.sharding import PartitionSpec as P

FRESNEL = 4.0
STEP_OBJECT = 0.5
STEP_PROBE = 0.5
ROWS = 8


def tables(points):
    position = np.arange(points)
    angle = -2.0 * np.pi / points * (position[:, None] * position[None, :] % points)
    dft = np.exp(1j * angle) / math.sqrt(points)
    frequency = np.where(position < points // 2, position, position - points) / points
    propagator = np.conj(dft) @ (np.exp(-1j * np.pi * FRESNEL * frequency**2)[:, None] * dft)

    def split(matrix):
        high = matrix.astype(np.float32).astype(ml_dtypes.bfloat16)
        low = (matrix - high.astype(np.float64)).astype(np.float32).astype(ml_dtypes.bfloat16)
        return high, low

    lefts, rights = [], []
    for matrix in (propagator, np.conj(propagator), dft, np.conj(dft)):
        real, imag = matrix.real, matrix.imag
        high, low = split(np.block([[real, -imag], [imag, real]]))
        lefts.append(np.concatenate([high, high, low], axis=1))
        high, low = split(np.block([[real, imag], [-imag, real]]))
        rights.append(np.concatenate([high, high, low], axis=0))
    return np.stack(lefts), np.stack(rights)


def split(value):
    high = value.astype(jnp.bfloat16)
    return high, (value - high.astype(jnp.float32)).astype(jnp.bfloat16)


def grid(blocks):
    return jnp.concatenate([jnp.concatenate(row, axis=1) for row in blocks], axis=0)


def left_product(weight, pair):
    n = pair[0].shape[0]
    (r0, r0l), (r1, r1l), (i0, i0l), (i1, i1l) = map(split, pair)
    x = grid([[r0, r1], [i0, i1], [r0l, r1l], [i0l, i1l], [r0, r1], [i0, i1]])
    y = jnp.dot(weight, x, preferred_element_type=jnp.float32)
    return y[:n, :n], y[:n, n:], y[n:, :n], y[n:, n:]


def right_product(weight, pair):
    n = pair[0].shape[0]
    (r0, r0l), (r1, r1l), (i0, i0l), (i1, i1l) = map(split, pair)
    x = grid([[r0, i0, r0l, i0l, r0, i0], [r1, i1, r1l, i1l, r1, i1]])
    y = jnp.dot(x, weight, preferred_element_type=jnp.float32)
    return y[:n, :n], y[n:, :n], y[:n, n:], y[n:, n:]


def times(pair, obj):
    (r0, r1, i0, i1), (a, b) = pair, obj
    return r0 * a - i0 * b, r1 * a - i1 * b, r0 * b + i0 * a, r1 * b + i1 * a


def times_conj(pair, obj):
    return times(pair, (obj[0], -obj[1]))


def remote(source, target, send, recv, device):
    return pltpu.make_async_remote_copy(
        src_ref=source, dst_ref=target, send_sem=send, recv_sem=recv,
        device_id=device, device_id_type=pl.DeviceIdType.MESH,
    )


def signal(device):
    pl.semaphore_signal(
        pltpu.get_barrier_semaphore(), inc=1, device_id=device, device_id_type=pl.DeviceIdType.MESH
    )


def step(
    n_row, n_col, counts, offsets, obj, probe, amplitudes, lefts, rights, new_object, new_probe,
    ext0, ext1, ext2, ext3, acc, window, waves, side_in, edge_in, low_in, sums, first, middle, second, total,
    load, send, recv, col_send, col_recv, row_send, row_recv,
):
    a, b = lax.axis_index("row"), lax.axis_index("col")
    ext = (ext0, ext1, ext2, ext3)
    depth, rows, cols = obj.shape[1:]
    modes, n = probe.shape[1:3]
    pairs = modes // 2
    slots = amplitudes.shape[0]
    big = middle.shape[0]
    small = big // n_row
    has_up, has_down, has_left, has_right = a > 0, a < n_row - 1, b > 0, b < n_col - 1
    up, down, left, right = (a - 1, b), (a + 1, b), (a, b - 1), (a, b + 1)
    tile_r, tile_c, rim_r, rim_c = pl.ds(0, rows), pl.ds(0, cols), pl.ds(rows, n), pl.ds(cols, n)
    head = pl.ds(0, n)

    loads = [pltpu.make_async_copy(obj.at[:, s], ext[s].at[:, tile_r, tile_c], load.at[s]) for s in range(depth)]
    for copy in loads:
        copy.start()
    col_peers = [lax.rem(b + i, n_col) for i in range(1, n_col)]
    row_peers = [lax.rem(a + i, n_row) for i in range(1, n_row)]
    for peer in col_peers:
        signal((a, peer))
    for peer in row_peers:
        signal((peer, b))
    pl.semaphore_wait(pltpu.get_barrier_semaphore(), n_col - 1 + n_row - 1)

    def copies(kind, device, ends):
        return [remote(*ends(s), send.at[kind, s], recv.at[kind, s], device) for s in range(depth)]

    rows_out = copies(0, up, lambda s: (obj.at[:, s, head, :], ext[s].at[:, rim_r, tile_c]))
    side_out = copies(1, left, lambda s: (obj.at[:, s, :, head], ext[s].at[:, tile_r, rim_c]))
    edge_out = copies(2, left, lambda s: (ext[s].at[:, rim_r, head], ext[s].at[:, rim_r, rim_c]))
    side_back = copies(3, right, lambda s: (acc.at[:, s, tile_r, rim_c], side_in.at[:, s]))
    edge_back = copies(4, right, lambda s: (acc.at[:, s, rim_r, rim_c], edge_in.at[:, s]))
    rows_back = copies(5, down, lambda s: (acc.at[:, s, rim_r, tile_c], low_in.at[:, s]))

    for s in range(depth):

        @pl.when(has_up)
        def _():
            rows_out[s].start()

        @pl.when(has_left)
        def _():
            side_out[s].start()

    sums[...] = jnp.zeros_like(sums)

    acc[...] = jnp.zeros_like(acc)

    @pl.when(jnp.logical_not(has_down))
    def _():
        for ref in ext:
            ref[:, rim_r, tile_c] = jnp.zeros((2, n, cols), jnp.float32)

    @pl.when(jnp.logical_not(has_right))
    def _():
        for ref in ext:
            ref[:, tile_r, rim_c] = jnp.zeros((2, rows, n), jnp.float32)

    @pl.when(jnp.logical_not(has_down & has_right))
    def _():
        for ref in ext:
            ref[:, rim_r, rim_c] = jnp.zeros((2, n, n), jnp.float32)

    tall = n + ROWS
    lane = lax.broadcasted_iota(jnp.int32, (tall, n), 1)

    def place(k):
        return offsets[0, 0, k, 0] - a * rows, offsets[0, 0, k, 1] - b * cols

    def alive(k):
        return jnp.minimum(jnp.maximum(counts[0, 0] - k, 0), 1).astype(jnp.float32)

    def pick(amount, bit, clear, taken):
        return jnp.where(((jnp.zeros(clear.shape, jnp.int32) + amount) & bit) != 0, taken, clear)

    def turn(value, amount, axis, limit, sign):
        bit = 1
        while bit < limit:
            value = pick(amount, bit, value, pltpu.roll(value, sign * bit % value.shape[axis], axis))
            bit *= 2
        return value

    def keep(k, level, state):
        for p in range(pairs):
            for c in range(2):
                for j in range(2):
                    waves[k, level, c, 2 * p + j] = state[p][2 * c + j]

    def kept(k, level):
        source = probe if level < 0 else waves.at[k, level]
        return [tuple(source[c, 2 * p + j] for c in range(2) for j in range(2)) for p in range(pairs)]

    def product(which, state):
        state = [left_product(lefts[which], pair) for pair in state]
        return [right_product(rights[which], pair) for pair in state]

    def digits(low, size):
        return [low << i for i in range((size // low - 1).bit_length())]

    def cut(k, s):
        y, x = place(k)
        near = lane >= (jnp.zeros(lane.shape, jnp.int32) + x) & (n - 1)
        for c in range(2):
            value = ext[s][c]
            for bit in reversed(digits(n, cols)):
                value = pick(x, bit, value[:, :-bit], value[:, bit:])
            for bit in reversed(digits(ROWS, rows)):
                value = pick(y, bit, value[:-bit], value[bit:])
            value = turn(jnp.where(near, value[:, :n], value[:, n:]), x, 1, n, -1)
            window[k, c, s] = turn(value, y, 0, ROWS, -1)[:n]

    def scatter(k, c, s, grad):
        y, x = place(k)
        near = lane >= (jnp.zeros(lane.shape, jnp.int32) + x) & (n - 1)
        value = jnp.concatenate([grad, jnp.zeros((ROWS, n), jnp.float32)], axis=0)
        value = turn(turn(value, y, 0, ROWS, 1), x, 1, n, 1)
        value = jnp.concatenate([jnp.where(near, value, 0.0), jnp.where(near, 0.0, value)], axis=1)
        for bit in digits(ROWS, rows):
            gap = jnp.zeros((bit, value.shape[1]), jnp.float32)
            value = pick(y, bit, jnp.concatenate([value, gap], axis=0), jnp.concatenate([gap, value], axis=0))
        for bit in digits(n, cols):
            gap = jnp.zeros((value.shape[0], bit), jnp.float32)
            value = pick(x, bit, jnp.concatenate([value, gap], axis=1), jnp.concatenate([gap, value], axis=1))
        acc[c, s] += value

    def back(k, s, state):
        grads = [0.0, 0.0]
        for g, w in zip(state, kept(k, s - 1)):
            for j in range(2):
                grads[0] += g[j] * w[j] + g[2 + j] * w[2 + j]
                grads[1] += g[2 + j] * w[j] - g[j] * w[2 + j]
        for c in range(2):
            scatter(k, c, s, grads[c] * STEP_OBJECT)
        state = [times_conj(pair, (window[k, 0, s], window[k, 1, s])) for pair in state]
        if s > 0:
            keep(k, depth - 1, state)
        else:
            for p in range(pairs):
                for c in range(2):
                    for j in range(2):
                        sums[pl.ds((c * modes + 2 * p + j) * n, n)] += state[p][2 * c + j]

    def pass_down(s):
        @pl.when(has_down & has_left)
        def _():
            edge_back[s].wait_recv()
            acc[:, s, rim_r, head] += edge_in[:, s]

        @pl.when(has_down)
        def _():
            rows_back[s].start()

    for s in range(depth):
        loads[s].wait()

        @pl.when(has_down)
        def _():
            rows_out[s].wait_recv()

        @pl.when(has_down & has_left)
        def _():
            edge_out[s].start()

        @pl.when(has_right)
        def _():
            side_out[s].wait_recv()

        @pl.when(has_down & has_right)
        def _():
            edge_out[s].wait_recv()

        @pl.loop(0, slots)
        def _(k):
            cut(k, s)
            o = (window[k, 0, s], window[k, 1, s])
            if s == 0:
                sums[pl.ds(2 * modes * n, n)] += alive(k) * (o[0] ** 2 + o[1] ** 2)
            state = [times(pair, o) for pair in kept(k, s - 1)]
            if s < depth - 1:
                keep(k, s, product(0, state))
            else:
                state = product(2, state)
                intensity = sum(v * v for pair in state for v in pair)
                factor = alive(k) * (2.0 - 2.0 * amplitudes[k] / jnp.sqrt(intensity + 1.0))
                state = [tuple(v * factor for v in pair) for pair in state]
                back(k, s, product(3, state))

    for s in range(depth - 1, -1, -1):
        if s < depth - 1:

            @pl.loop(0, slots)
            def _(k):
                back(k, s, product(1, kept(k, depth - 1)))

            pass_down(s + 1)

        @pl.when(has_down & has_right)
        def _():
            edge_back[s].start()

        if s > 0:

            @pl.when(has_right)
            def _():
                side_back[s].start()

    def chunk(ref, index, size):
        return ref.at[pl.ds(pl.multiple_of(index * size, ROWS), size)]

    scatter_col = [
        remote(chunk(sums, peer, big), first.at[i], col_send.at[0, i], col_recv.at[0, i], (a, peer))
        for i, peer in enumerate(col_peers)
    ]
    for copy in scatter_col:
        copy.start()

    @pl.when(has_right)
    def _():
        side_back[0].start()

    pass_down(0)
    for s in range(depth):
        new_object[:, s] = ext[s][:, tile_r, tile_c] - acc[:, s, tile_r, tile_c]
    for copy in scatter_col:
        copy.wait()
    mine = chunk(sums, b, big)[...]
    for i in range(n_col - 1):
        mine += first[i]
    middle[...] = mine
    scatter_row = [
        remote(chunk(middle, peer, small), second.at[i], row_send.at[0, i], row_recv.at[0, i], (peer, b))
        for i, peer in enumerate(row_peers)
    ]
    for copy in scatter_row:
        copy.start()
    for copy in scatter_row:
        copy.wait()
    mine = chunk(middle, a, small)[...]
    for i in range(n_row - 1):
        mine += second[i]
    own = chunk(total, b * n_row + a, small)
    own[...] = mine
    gather_row = [
        remote(own, own, row_send.at[1, i], row_recv.at[1, i], (peer, b)) for i, peer in enumerate(row_peers)
    ]
    for copy in gather_row:
        copy.start()
    for copy in gather_row:
        copy.wait()
    group = chunk(total, b, big)
    gather_col = [
        remote(group, group, col_send.at[1, i], col_recv.at[1, i], (a, peer)) for i, peer in enumerate(col_peers)
    ]
    for copy in gather_col:
        copy.start()

    for s in range(depth - 1, -1, -1):

        @pl.when(has_left)
        def _():
            side_back[s].wait_recv()
            new_object[:, s, :, head] -= side_in[:, s]

        @pl.when(has_up)
        def _():
            rows_back[s].wait_recv()
            new_object[:, s, head, :] -= low_in[:, s]

    for copy in gather_col:
        copy.wait()
    scale = STEP_PROBE / (total[pl.ds(2 * modes * n, n)] + 1.0)
    for c in range(2):
        for m in range(modes):
            new_probe[c, m] = probe[c, m] - total[pl.ds((c * modes + m) * n, n)] * scale

    for s in range(depth):

        @pl.when(has_up)
        def _():
            rows_out[s].wait_send()

        @pl.when(has_left)
        def _():
            side_out[s].wait_send()

        @pl.when(has_down & has_left)
        def _():
            edge_out[s].wait_send()

        @pl.when(has_right)
        def _():
            side_back[s].wait_send()

        @pl.when(has_down & has_right)
        def _():
            edge_back[s].wait_send()

        @pl.when(has_down)
        def _():
            rows_back[s].wait_send()


def shards(n_row, n_col, object_field, probe, amplitudes, offsets, counts):
    _, depth, rows, cols = object_field.shape
    modes, n = probe.shape[1:3]
    slots = amplitudes.shape[2]
    f32 = jnp.float32
    vmem = pl.BlockSpec(memory_space=pltpu.VMEM)
    smem = pl.BlockSpec(memory_space=pltpu.SMEM)
    hbm = pl.BlockSpec(memory_space=pl.ANY)
    dma = pltpu.SemaphoreType.DMA
    lefts, rights = tables(n)
    devices = n_row * n_col
    small = -(-(2 * modes + 1) * n // (devices * ROWS)) * ROWS
    flops = slots * depth * 4 * 2 * (modes * n) * (6 * n) * (2 * n)
    return pl.pallas_call(
        partial(step, n_row, n_col),
        out_shape=(
            jax.ShapeDtypeStruct(object_field.shape, f32),
            jax.ShapeDtypeStruct(probe.shape, f32),
        ),
        in_specs=[smem, smem, hbm, vmem, vmem, vmem, vmem],
        out_specs=(vmem, vmem),
        scratch_shapes=[
            *[pltpu.VMEM((2, rows + n, cols + n), f32)] * 4,
            pltpu.VMEM((2, depth, rows + n, cols + n), f32),
            pltpu.VMEM((slots, 2, depth, n, n), f32),
            pltpu.VMEM((slots, depth, 2, modes, n, n), f32),
            pltpu.VMEM((2, depth, rows, n), f32),
            pltpu.VMEM((2, depth, n, n), f32),
            pltpu.VMEM((2, depth, n, cols), f32),
            pltpu.VMEM((devices * small, n), f32),
            pltpu.VMEM((n_col - 1, n_row * small, n), f32),
            pltpu.VMEM((n_row * small, n), f32),
            pltpu.VMEM((n_row - 1, small, n), f32),
            pltpu.VMEM((devices * small, n), f32),
            dma((depth,)),
            dma((6, depth)),
            dma((6, depth)),
            dma((2, n_col - 1)),
            dma((2, n_col - 1)),
            dma((2, n_row - 1)),
            dma((2, n_row - 1)),
        ],
        compiler_params=pltpu.CompilerParams(
            collective_id=0, has_side_effects=True, vmem_limit_bytes=56 * 2**20
        ),
        cost_estimate=pl.CostEstimate(flops=flops, bytes_accessed=8 * 2**20, transcendentals=0),
        name="step",
    )(counts, offsets, object_field, probe, amplitudes[0, 0], jnp.asarray(lefts), jnp.asarray(rights))


def solution(mesh):
    return jax.shard_map(
        partial(shards, mesh.shape["row"], mesh.shape["col"]),
        mesh=mesh,
        in_specs=(
            P(None, None, "row", "col"),
            P(),
            P("row", "col", None, None, None),
            P("row", "col", None, None),
            P("row", "col"),
        ),
        out_specs=(P(None, None, "row", "col"), P()),
        check_vma=False,
    )
```

time: 235 us -> 118 us (0.50)
  waiting for transfers between devices: 154 us -> 0 us
  Pallas kernels: 31 us -> 112 us
  starting transfers between devices: 21.4 us -> 0 us
  between operations: 14.8 us -> 1.29 us
  other arithmetic: 6.25 us -> 0 us
    psum x1 -> x0, waiting for transfers between devices: 121 us -> none  [shards(): totals = lax.psum(sums, ('row', 'col'))]
    pallas_call x1, Pallas kernels: 31 us -> 112 us  [shards(): pl.pallas_call(partial(step, n_row, n_col), out_shape=(jax.ShapeDtypeStru...]
    ppermute x6 -> x0, waiting for transfers between devices: 32.6 us -> none  [shift(): return lax.ppermute(value, ('row', 'col'), pairs)]
    ppermute x6 -> x0, starting transfers between devices: 21.4 us -> none  [shift(): return lax.ppermute(value, ('row', 'col'), pairs)]
    sub x2 -> x0, other arithmetic: 4.17 us -> none  [the longest x1 3.32 us: shards(): new_object = part - widen(low) - widen(side) - widen(edge)]
    slice x3 -> x0, local copies, waits for them, and re-layouts: 3.33 us -> none  [the longest x1 1.45 us: shards(): below = shift(object_field[:, :, :n, :], 1, 0, 1)]
    unnamed x19 -> x5, local copies, waits for them, and re-layouts: 4.14 us -> 5.25 us
  transfers between devices with their start and end apart: 7 -> 0, of which waited for: 2 -> 0; matrix products, arithmetic and copies ran while one was open for 2% -> 0% of each run, Pallas kernels for 0% -> 0%
where the time goes in v3:
time: 118 us
  Pallas kernels  112 us (95%)
  local copies, waits for them, and re-layouts  5.25 us (4%)
  between operations  1.29 us (1%)
    pallas_call x1, Pallas kernels, shards(): pl.pallas_call(partial(step, n_row, n_col), out_shape=(jax.ShapeDtypeStru...  112 us
    unnamed x5, local copies, waits for them, and re-layouts  5.25 us

profile of v3, /device:TPU:1, one launch (start us, length us, event | category | flops | bytes accessed | tf_op | source)
XLA Modules:
  0.0 118.3 jit_solution(18009757835093177117)
XLA Ops:
  1.3 1.4 %copy.9.offsets = s32[1,1,5,2]{3,2,1,0:T(8,128)} copy(s32[1,1,5,2]{2,3,1,0:T(2,128)} %param.10) | data formatting | bytes 80 | tf_op args[3]
  2.6 111.8 %step.1 = (f32[2,4,256,256]{3,2,1,0:T(8,128)}, f32[2,4,128,128]{3,2,1,0:T(8,128)}) custom-call(s32[1,1]{1,0:T(1,128)S(6)} %copy.12.counts, s32[1,1,5,2]{3,2,1,0:T(8,128)} %copy.9.offsets, f32[2,4,256,256]{3,2,1,0:T(8,128)} %obj.1, f32[2,4,128,128]{3,2,1,0:T(8,128)} %probe.1, f32[5,128,128]{2,1,0:T(8,128)} %bitcast.1, ...), custom_call_target="tpu_custom_call" | custom-call | flops 16106127360 | bytes 8388608 | tf_op jit(solution)/shard_map/step/pallas_call | solution.py:408
  114.4 0.0 copy-start
  114.4 3.1 %copy.13 = f32[2,4,256,256]{3,2,1,0:T(8,128)} copy(f32[2,4,256,256]{3,2,1,0:T(8,128)} %get-tuple-element.4) | data formatting | bytes 4194304
  117.5 0.0 copy-done
  117.5 0.8 copy.14
Async XLA Ops:
  114.4 3.1 %copy-start = (f32[2,4,128,128]{3,2,1,0:T(8,128)S(1)}, f32[2,4,128,128]{3,2,1,0:T(8,128)}, u32[]{:S(2)}) copy-start(f32[2,4,128,128]{3,2,1,0:T(8,128)} %get-tuple-element.5) | copy-start | bytes 1572868

commit v4 on v3

--- a/solution.py
+++ b/solution.py
@@ -87,7 +87,7 @@
 
 def step(
     n_row, n_col, counts, offsets, obj, probe, amplitudes, lefts, rights, new_object, new_probe,
-    ext0, ext1, ext2, ext3, acc, window, waves, side_in, edge_in, low_in, sums, first, middle, second, total,
+    ext0, ext1, ext2, ext3, acc, window, waves, flat, pad, side_in, edge_in, low_in, sums, first, middle, second, total,
     load, send, recv, col_send, col_recv, row_send, row_recv,
 ):
     a, b = lax.axis_index("row"), lax.axis_index("col")
@@ -136,7 +136,10 @@
 
     sums[...] = jnp.zeros_like(sums)
 
-    acc[...] = jnp.zeros_like(acc)
+
+    @pl.loop(0, slots)
+    def _(k):
+        pad[k] = jnp.zeros_like(pad[k])
 
     @pl.when(jnp.logical_not(has_down))
     def _():
@@ -154,10 +157,11 @@
             ref[:, rim_r, rim_c] = jnp.zeros((2, n, n), jnp.float32)
 
     tall = n + ROWS
+    lead = rows // ROWS - 1
     lane = lax.broadcasted_iota(jnp.int32, (tall, n), 1)
 
     def place(k):
-        return offsets[0, 0, k, 0] - a * rows, offsets[0, 0, k, 1] - b * cols
+        return lax.rem(offsets[0, 0, k, 0], rows), lax.rem(offsets[0, 0, k, 1], cols)
 
     def alive(k):
         return jnp.minimum(jnp.maximum(counts[0, 0] - k, 0), 1).astype(jnp.float32)
@@ -186,34 +190,43 @@
         state = [left_product(lefts[which], pair) for pair in state]
         return [right_product(rights[which], pair) for pair in state]
 
-    def digits(low, size):
-        return [low << i for i in range((size // low - 1).bit_length())]
-
     def cut(k, s):
         y, x = place(k)
         near = lane >= (jnp.zeros(lane.shape, jnp.int32) + x) & (n - 1)
+        tile, block = lax.div(y, ROWS), lax.div(x, n)
         for c in range(2):
-            value = ext[s][c]
-            for bit in reversed(digits(n, cols)):
-                value = pick(x, bit, value[:, :-bit], value[:, bit:])
-            for bit in reversed(digits(ROWS, rows)):
-                value = pick(y, bit, value[:-bit], value[bit:])
-            value = turn(jnp.where(near, value[:, :n], value[:, n:]), x, 1, n, -1)
+            first_block = jnp.concatenate([flat[c, block, tile + i] for i in range(tall // ROWS)], axis=0)
+            next_block = jnp.concatenate([flat[c, block + 1, tile + i] for i in range(tall // ROWS)], axis=0)
+            value = turn(jnp.where(near, first_block, next_block), x, 1, n, -1)
             window[k, c, s] = turn(value, y, 0, ROWS, -1)[:n]
 
     def scatter(k, c, s, grad):
         y, x = place(k)
-        near = lane >= (jnp.zeros(lane.shape, jnp.int32) + x) & (n - 1)
+        corner = jnp.zeros(lane.shape, jnp.int32) + x
+        near = lane >= corner & (n - 1)
+        block = corner - (corner & (n - 1)) + jnp.where(near, 0, n)
         value = jnp.concatenate([grad, jnp.zeros((ROWS, n), jnp.float32)], axis=0)
         value = turn(turn(value, y, 0, ROWS, 1), x, 1, n, 1)
-        value = jnp.concatenate([jnp.where(near, value, 0.0), jnp.where(near, 0.0, value)], axis=1)
-        for bit in digits(ROWS, rows):
-            gap = jnp.zeros((bit, value.shape[1]), jnp.float32)
-            value = pick(y, bit, jnp.concatenate([value, gap], axis=0), jnp.concatenate([gap, value], axis=0))
-        for bit in digits(n, cols):
-            gap = jnp.zeros((value.shape[0], bit), jnp.float32)
-            value = pick(x, bit, jnp.concatenate([value, gap], axis=1), jnp.concatenate([gap, value], axis=1))
-        acc[c, s] += value
+        value = jnp.concatenate([jnp.where(block == start, value, 0.0) for start in range(0, cols + n, n)], axis=1)
+        for i in range(tall // ROWS):
+            pad[k, c, lead + i] = value[i * ROWS : (i + 1) * ROWS]
+
+    def flatten(s):
+        for c in range(2):
+            for j in range((cols + n) // n):
+                flat[c, j] = ext[s][c, :, j * n : (j + 1) * n].reshape((rows + n) // ROWS, ROWS, n)
+
+    def add_up(s):
+        starts = [lead - lax.div(place(k)[0], ROWS) for k in range(slots)]
+
+        @pl.loop(0, (rows + n) // (4 * ROWS))
+        def _(i):
+            for c in range(2):
+                for t in range(4):
+                    value = pad[0, c, starts[0] + i * 4 + t]
+                    for k in range(1, slots):
+                        value += pad[k, c, starts[k] + i * 4 + t]
+                    acc[c, s, pl.ds(pl.multiple_of((i * 4 + t) * ROWS, ROWS), ROWS), :] = value
 
     def back(k, s, state):
         grads = [0.0, 0.0]
@@ -261,6 +274,8 @@
         def _():
             edge_out[s].wait_recv()
 
+        flatten(s)
+
         @pl.loop(0, slots)
         def _(k):
             cut(k, s)
@@ -285,6 +300,7 @@
                 back(k, s, product(1, kept(k, depth - 1)))
 
             pass_down(s + 1)
+        add_up(s)
 
         @pl.when(has_down & has_right)
         def _():
@@ -418,6 +434,8 @@
             pltpu.VMEM((2, depth, rows + n, cols + n), f32),
             pltpu.VMEM((slots, 2, depth, n, n), f32),
             pltpu.VMEM((slots, depth, 2, modes, n, n), f32),
+            pltpu.VMEM((2, (cols + n) // n, (rows + n) // ROWS, ROWS, n), f32),
+            pltpu.VMEM((slots, 2, (2 * rows + n) // ROWS - 1, ROWS, cols + n), f32),
             pltpu.VMEM((2, depth, rows, n), f32),
             pltpu.VMEM((2, depth, n, n), f32),
             pltpu.VMEM((2, depth, n, cols), f32),

time: 118 us -> 116 us (0.983)
  Pallas kernels: 112 us -> 110 us
    pallas_call x1, Pallas kernels: 112 us -> 110 us  [shards(): pl.pallas_call(partial(step, n_row, n_col), out_shape=(jax.ShapeDtypeStru...]
where the time goes in v4:
time: 116 us
  Pallas kernels  110 us (95%)
  local copies, waits for them, and re-layouts  5.25 us (5%)
  between operations  1.29 us (1%)
    pallas_call x1, Pallas kernels, shards(): pl.pallas_call(partial(step, n_row, n_col), out_shape=(jax.ShapeDtypeStru...  110 us
    unnamed x5, local copies, waits for them, and re-layouts  5.25 us

profile of v4, /device:TPU:1, one launch (start us, length us, event | category | flops | bytes accessed | tf_op | source)
XLA Modules:
  0.0 116.1 jit_solution(12815714850509611471)
XLA Ops:
  1.3 1.4 %copy.9.offsets = s32[1,1,5,2]{3,2,1,0:T(8,128)} copy(s32[1,1,5,2]{2,3,1,0:T(2,128)} %param.10) | data formatting | bytes 80 | tf_op args[3]
  2.6 109.5 %step.1 = (f32[2,4,256,256]{3,2,1,0:T(8,128)}, f32[2,4,128,128]{3,2,1,0:T(8,128)}) custom-call(s32[1,1]{1,0:T(1,128)S(6)} %copy.12.counts, s32[1,1,5,2]{3,2,1,0:T(8,128)} %copy.9.offsets, f32[2,4,256,256]{3,2,1,0:T(8,128)} %obj.1, f32[2,4,128,128]{3,2,1,0:T(8,128)} %probe.1, f32[5,128,128]{2,1,0:T(8,128)} %bitcast.1, ...), custom_call_target="tpu_custom_call" | custom-call | flops 16106127360 | bytes 8388608 | tf_op jit(solution)/shard_map/step/pallas_call | solution.py:424
  112.2 0.0 copy-start
  112.2 3.1 %copy.13 = f32[2,4,256,256]{3,2,1,0:T(8,128)} copy(f32[2,4,256,256]{3,2,1,0:T(8,128)} %get-tuple-element.4) | data formatting | bytes 4194304
  115.3 0.0 copy-done
  115.3 0.8 copy.14
Async XLA Ops:
  112.2 3.1 %copy-start = (f32[2,4,128,128]{3,2,1,0:T(8,128)S(1)}, f32[2,4,128,128]{3,2,1,0:T(8,128)}, u32[]{:S(2)}) copy-start(f32[2,4,128,128]{3,2,1,0:T(8,128)} %get-tuple-element.5) | copy-start | bytes 1572868
